TPU v7x, 256 devices: a whole 4x4x8 slice. The times are simulated.
256 devices in a mesh: depth: 8 (over z), height: 32 (over y, x, core).
Axes of the slice: x: 4, y: 4, z: 8, core: 2. Of those that a mesh axis runs over, the one named last changes fastest.
Arguments:
- volume: float32 [256, 256, 2048], P('depth', 'height'), may hold values from -6 to 6
- colour_coef: float32 [3, 4], replicated, may hold values from -4 to 4
- opacity_coef: float32 [4], replicated, may hold values from -4 to 4
- light_dir: float32 [4, 3], replicated, may hold values from -4 to 4
- light_colour: float32 [4, 3], replicated, may hold values from 0.2 to 1.5
Outputs:
- composite_image: float32 [13, 256, 2048], P(None, 'height')
All inputs are finite; a program needn't handle non-finite values.
Results may differ from a plain program's by a relative error of at most 0.00002.
Values sent between devices are 32-bit elements; how exact they have to be, the bound alone decides.
No kernel may reach another device: no remote copies, remote signals or barrier semaphores. Data moves between devices by JAX's collectives and lax.ppermute only.
A program may use at most 128 MiB of HBM per device.

v0:
```python
import jax
import jax.numpy as jnp
from jax import lax
from jax.sharding import PartitionSpec as P


def with_halo(cells, sides, width):
    for axis, dim in sides:
        count = lax.axis_size(axis)
        ends = count - 1
        head = lax.slice_in_dim(cells, 0, width, axis=dim)
        tail = lax.slice_in_dim(cells, cells.shape[dim] - width, cells.shape[dim], axis=dim)
        cells = jnp.concatenate(
            [
                lax.ppermute(tail, axis, [(i, (i + 1) % count) for i in range(ends)]),
                cells,
                lax.ppermute(head, axis, [((i + 1) % count, i) for i in range(ends)]),
            ],
            axis=dim,
        )
    return cells


def diffuse(padded):
    centre = padded[1:-1, 1:-1]
    widened = jnp.pad(centre, ((0, 0), (0, 0), (1, 1)))
    neighbours = (
        padded[2:, 1:-1],
        padded[:-2, 1:-1],
        padded[1:-1, 2:],
        padded[1:-1, :-2],
        widened[:, :, 2:],
        widened[:, :, :-2],
    )
    flux_sum = jnp.zeros_like(centre)
    for neighbour in neighbours:
        differ = neighbour - centre
        flux_sum = flux_sum + differ / (1.0 + differ * differ)
    return centre + 0.12 * flux_sum


def slopes(padded):
    centre = padded[1:-1, 1:-1]
    widened = jnp.pad(centre, ((0, 0), (0, 0), (1, 1)))
    return (
        0.5 * (padded[2:, 1:-1] - padded[:-2, 1:-1]),
        0.5 * (padded[1:-1, 2:] - padded[1:-1, :-2]),
        0.5 * (widened[:, :, 2:] - widened[:, :, :-2]),
    )


def shade(
    values,
    grad_depth,
    grad_height,
    grad_width,
    colour_coef,
    opacity_coef,
    light_dir,
    light_colour,
    alpha_top,
):
    squared = values * values
    cubed = squared * values
    base_colour = [
        0.5
        + 0.5
        * jnp.tanh(
            colour_coef[channel, 0]
            + colour_coef[channel, 1] * values
            + colour_coef[channel, 2] * squared
            + colour_coef[channel, 3] * cubed
        )
        for channel in range(3)
    ]
    polynomial = (
        opacity_coef[0]
        + opacity_coef[1] * values
        + opacity_coef[2] * squared
        + opacity_coef[3] * cubed
    )
    strength = polynomial * polynomial
    opacity = alpha_top * strength / (1.0 + strength)
    inverse = lax.rsqrt(
        grad_depth * grad_depth + grad_height * grad_height + grad_width * grad_width + 1.0
    )
    colours = []
    for light_index in range(4):
        facing = jnp.abs(
            inverse
            * (
                grad_depth * light_dir[light_index, 0]
                + grad_height * light_dir[light_index, 1]
                + grad_width * light_dir[light_index, 2]
            )
        )
        for channel in range(3):
            colours.append(
                base_colour[channel] * light_colour[light_index, channel] * (0.2 + facing)
            )
    return (jnp.stack(colours), opacity)


def render_slab(
    smooth,
    grad_depth,
    grad_height,
    grad_width,
    colour_coef,
    opacity_coef,
    light_dir,
    light_colour,
    alpha_top,
):
    colours, opacity = shade(
        smooth,
        grad_depth,
        grad_height,
        grad_width,
        colour_coef,
        opacity_coef,
        light_dir,
        light_colour,
        alpha_top,
    )
    remaining = jnp.cumprod(1.0 - opacity, axis=0)
    before = jnp.concatenate([jnp.ones_like(remaining[:1]), remaining[:-1]], 0)
    weights = before * opacity
    colour_sum = jnp.sum(weights[None] * colours, axis=1)
    return jnp.concatenate([colour_sum, (1.0 - remaining[-1])[None]], 0)


def over(front, back):
    return front + (1.0 - front[12:13]) * back


def per_device(volume, colour_coef, opacity_coef, light_dir, light_colour):
    depth_count = lax.axis_size("depth")
    slab_cells, band_rows, width_cells = volume.shape
    alpha_top = 2.0 / (slab_cells * depth_count)

    def with_rim(cells):
        return with_halo(cells, (("depth", 0), ("height", 1)), 1)

    smooth_one = diffuse(with_rim(volume))
    smooth_two = diffuse(with_rim(smooth_one))
    padded_two = with_rim(smooth_two)
    grad_depth, grad_height, grad_width = slopes(padded_two)
    partial_value = render_slab(
        smooth_two,
        grad_depth,
        grad_height,
        grad_width,
        colour_coef,
        opacity_coef,
        light_dir,
        light_colour,
        alpha_top,
    )
    gathered = lax.all_gather(partial_value, "depth", axis=0, tiled=True).reshape(
        depth_count, 13, band_rows, width_cells
    )
    forward = gathered[0]
    for slab_index in range(1, depth_count):
        forward = over(forward, gathered[slab_index])
    return forward


def solution(mesh):
    placed = (P("depth", "height", None), P(), P(), P(), P())
    return jax.shard_map(
        per_device, mesh=mesh, in_specs=placed, out_specs=P(None, "height", None), check_vma=False
    )
```

profile of v0, /device:TPU:1, one launch (start us, length us, event | category | flops | bytes accessed | tf_op | source)
XLA Modules:
  0.0 276.4 jit_solution(13851763492206103754)
XLA Ops:
  7.4 4.4 %collective-permute-start.1 = (f32[1,8,2048]{2,1,0:T(8,128)S(1)}, f32[1,8,2048]{2,1,0:T(8,128)S(1)}, u32[]{:S(2)}, u32[]{:S(2)}) collective-permute-start(f32[1,8,2048]{2,1,0:T(8,128)S(1)} %get-tuple-element.18), channel_id=1, source_target_pairs={{0,32},{32,64},{64,96},{96,128},{128,160},{160,192},{192,224},{1,3... | collective-permute-start | bytes 196616 | tf_op jit(solution)/shard_map/ppermute | solution.py:15
  17.4 3.8 %collective-permute-start.2 = (f32[34,1,2048]{2,1,0:T(1,128)S(1)}, f32[34,1,2048]{2,1,0:T(1,128)S(1)}, u32[]{:S(2)}, u32[]{:S(2)}) collective-permute-start(f32[34,1,2048]{2,1,0:T(1,128)S(1)} %get-tuple-element.11), channel_id=1, source_target_pairs={{1,0},{2,1},{3,2},{4,3},{5,4},{6,5},{7,6},{8,7},{9,8},{10,9},{11,1... | collective-permute-start | bytes 835592 | tf_op jit(solution)/shard_map/ppermute | solution.py:17
  27.7 4.4 %multiply_add_fusion.1 = f32[32,8,2048]{2,1,0:T(8,128)S(1)} fusion(f32[32,8,2048]{2,1,0:T(8,128)S(1)} %copy-done.1, f32[34,8,2048]{2,1,0:T(8,128)S(1)} %constant_dynamic-update-slice_fusion, f32[34,1,2048]{2,1,0:T(1,128)S(1)} %collective-permute-done.3, f32[34,1,2048]{2,1,0:T(1,128)S(1)} %collective-permute-done.2, ...), kind=kLoop, calls=%fused_computation.87 | loop fusion | flops 18350080 | bytes 7110656 | tf_op jit(solution)/shard_map/add | solution.py:39
  37.7 4.3 %collective-permute-done.4 = f32[1,8,2048]{2,1,0:T(8,128)S(1)} collective-permute-done((f32[1,8,2048]{2,1,0:T(8,128)S(1)}, f32[1,8,2048]{2,1,0:T(8,128)S(1)}, u32[]{:S(2)}, u32[]{:S(2)}) %collective-permute-start.4) | collective-permute-done | bytes 65568 | tf_op jit(solution)/shard_map/ppermute | solution.py:17
  44.3 5.5 %collective-permute-start.7 = (f32[34,1,2048]{2,1,0:T(1,128)S(1)}, f32[34,1,2048]{2,1,0:T(1,128)S(1)}, u32[]{:S(2)}, u32[]{:S(2)}) collective-permute-start(f32[34,1,2048]{2,1,0:T(1,128)S(1)} %get-tuple-element.10), channel_id=1, source_target_pairs={{0,1},{1,2},{2,3},{3,4},{4,5},{5,6},{6,7},{7,8},{8,9},{9,10},{10,1... | collective-permute-start | bytes 835592 | tf_op jit(solution)/shard_map/ppermute | solution.py:15
  59.5 5.4 %multiply_add_fusion = f32[32,8,2048]{2,1,0:T(8,128)S(1)} fusion(f32[32,8,2048]{2,1,0:T(8,128)S(1)} %multiply_add_fusion.1, f32[1,8,2048]{2,1,0:T(8,128)S(1)} %collective-permute-done.4, f32[1,8,2048]{2,1,0:T(8,128)S(1)} %collective-permute-done.5, f32[34,1,2048]{2,1,0:T(1,128)S(1)} %collective-permute-done.7, f32[34,1,2048]{2,1,0:T(1,128)S(1)} %collective-permute-done.6), kind=kLoop, calls=%fused_computation.86 | loop fusion | flops 20447232 | bytes 4882432 | tf_op jit(solution)/shard_map/add | solution.py:39
  64.9 4.9 %collective-permute-start.9 = (f32[1,8,2048]{2,1,0:T(8,128)S(1)}, f32[1,8,2048]{2,1,0:T(8,128)S(1)}, u32[]{:S(2)}, u32[]{:S(2)}) collective-permute-start(f32[1,8,2048]{2,1,0:T(8,128)S(1)} %get-tuple-element.13), channel_id=1, source_target_pairs={{0,32},{32,64},{64,96},{96,128},{128,160},{160,192},{192,224},{1,3... | collective-permute-start | bytes 196616 | tf_op jit(solution)/shard_map/ppermute | solution.py:15
  71.1 4.1 %fusion.33 = f32[32,8,2048]{2,1,0:T(8,128)S(1)} fusion(f32[32,8,2048]{2,1,0:T(8,128)S(1)} %multiply_add_fusion, f32[]{:T(128)} %bitcast.3, f32[]{:T(128)} %bitcast.2, f32[]{:T(128)} %bitcast.1, f32[]{:T(128)} %bitcast), kind=kOutput, calls=%fused_computation.83 | output fusion | flops 23068672 | bytes 4194320 | tf_op jit(solution)/shard_map/jit(cumprod)/reduce_window | solution.py:126
  75.3 8.9 %pad_multiply_fusion = f32[32,8,2048]{2,1,0:T(8,128)S(1)} fusion(f32[31,8,2048]{2,1,0:T(8,128)S(1)} %slice.373, f32[]{:T(128)} %bitcast.3, f32[]{:T(128)} %bitcast.2, f32[]{:T(128)} %bitcast.1, f32[]{:T(128)} %bitcast, f32[32,8,2048]{2,1,0:T(8,128)S(1)} %multiply_add_fusion.1, f32[1,8,2048]{2,1,0:T(8,128)S(1)} %collective-permute-done.4, ...), kind=kLoop, calls=%fused_computation.82 | loop fusion | flops 27262976 | bytes 6914064 | tf_op jit(solution)/shard_map/mul | solution.py:128
  86.5 3.8 %collective-permute-start.11 = (f32[34,1,2048]{2,1,0:T(1,128)S(1)}, f32[34,1,2048]{2,1,0:T(1,128)S(1)}, u32[]{:S(2)}, u32[]{:S(2)}) collective-permute-start(f32[34,1,2048]{2,1,0:T(1,128)S(1)} %get-tuple-element.8), channel_id=1, source_target_pairs={{0,1},{1,2},{2,3},{3,4},{4,5},{5,6},{6,7},{7,8},{8,9},{9,10},{10,1... | collective-permute-start | bytes 835592 | tf_op jit(solution)/shard_map/ppermute | solution.py:15
  93.7 8.1 %bitcast_dynamic-update-slice_fusion.11 = (f32[12,32,8,2048]{3,2,1,0:T(8,128)S(1)}, f32[32,8,2048]{2,1,0:T(8,128)S(1)}) fusion(f32[]{:T(128)} %bitcast.8, f32[32,8,2048]{2,1,0:T(8,128)S(1)} %multiply_add_fusion, f32[]{:T(128)} %bitcast.7, f32[]{:T(128)} %bitcast.6, f32[]{:T(128)} %bitcast.5, f32[]{:T(128)} %bitcast.4, f32[]{:T(128)} %bitcast.11, ...), kind=kLoop, calls=%fused_computation.76 | loop fusion | flops 20971520 | bytes 6979616
  101.7 6.3 %bitcast_dynamic-update-slice_fusion.10 = f32[12,32,8,2048]{3,2,1,0:T(8,128)S(1)} fusion(f32[12,32,8,2048]{3,2,1,0:T(8,128)S(1)} %get-tuple-element.5, f32[]{:T(128)} %bitcast.17, f32[32,8,2048]{2,1,0:T(8,128)S(1)} %multiply_add_fusion, f32[]{:T(128)} %bitcast.16, f32[]{:T(128)} %bitcast.15, f32[]{:T(128)} %bitcast.14, f32[]{:T(128)} %bitcast.13, ...), kind=kLoop, calls=%fused_computation.75 | loop fusion | flops 20447232 | bytes 6979616
  108.0 6.3 %bitcast_dynamic-update-slice_fusion.9 = f32[12,32,8,2048]{3,2,1,0:T(8,128)S(1)} fusion(f32[12,32,8,2048]{3,2,1,0:T(8,128)S(1)} %bitcast_dynamic-update-slice_fusion.10, f32[]{:T(128)} %bitcast.23, f32[32,8,2048]{2,1,0:T(8,128)S(1)} %multiply_add_fusion, f32[]{:T(128)} %bitcast.22, f32[]{:T(128)} %bitcast.21, f32[]{:T(128)} %bitcast.20, f32[]{:T(128)} %bitcast.19, ...), kind=kLoop, calls=%fused_computation.74 | loop fusion | flops 20447232 | bytes 6979616
  114.3 6.3 %bitcast_dynamic-update-slice_fusion.8 = f32[12,32,8,2048]{3,2,1,0:T(8,128)S(1)} fusion(f32[12,32,8,2048]{3,2,1,0:T(8,128)S(1)} %bitcast_dynamic-update-slice_fusion.9, f32[]{:T(128)} %bitcast.25, f32[32,8,2048]{2,1,0:T(8,128)S(1)} %multiply_add_fusion, f32[]{:T(128)} %bitcast.7, f32[]{:T(128)} %bitcast.6, f32[]{:T(128)} %bitcast.5, f32[]{:T(128)} %bitcast.4, ...), kind=kLoop, calls=%fused_computation.73 | loop fusion | flops 20447232 | bytes 6979616
  120.6 6.1 %bitcast_dynamic-update-slice_fusion.7 = f32[12,32,8,2048]{3,2,1,0:T(8,128)S(1)} fusion(f32[12,32,8,2048]{3,2,1,0:T(8,128)S(1)} %bitcast_dynamic-update-slice_fusion.8, f32[]{:T(128)} %bitcast.30, f32[32,8,2048]{2,1,0:T(8,128)S(1)} %multiply_add_fusion, f32[]{:T(128)} %bitcast.16, f32[]{:T(128)} %bitcast.15, f32[]{:T(128)} %bitcast.14, f32[]{:T(128)} %bitcast.13, ...), kind=kLoop, calls=%fused_computation.72 | loop fusion | flops 20447232 | bytes 6979616
  126.7 6.2 %bitcast_dynamic-update-slice_fusion.6 = f32[12,32,8,2048]{3,2,1,0:T(8,128)S(1)} fusion(f32[12,32,8,2048]{3,2,1,0:T(8,128)S(1)} %bitcast_dynamic-update-slice_fusion.7, f32[]{:T(128)} %bitcast.32, f32[32,8,2048]{2,1,0:T(8,128)S(1)} %multiply_add_fusion, f32[]{:T(128)} %bitcast.22, f32[]{:T(128)} %bitcast.21, f32[]{:T(128)} %bitcast.20, f32[]{:T(128)} %bitcast.19, ...), kind=kLoop, calls=%fused_computation.71 | loop fusion | flops 20447232 | bytes 6979616
  133.0 6.4 %bitcast_dynamic-update-slice_fusion.5 = f32[12,32,8,2048]{3,2,1,0:T(8,128)S(1)} fusion(f32[12,32,8,2048]{3,2,1,0:T(8,128)S(1)} %bitcast_dynamic-update-slice_fusion.6, f32[]{:T(128)} %bitcast.34, f32[32,8,2048]{2,1,0:T(8,128)S(1)} %multiply_add_fusion, f32[]{:T(128)} %bitcast.7, f32[]{:T(128)} %bitcast.6, f32[]{:T(128)} %bitcast.5, f32[]{:T(128)} %bitcast.4, ...), kind=kLoop, calls=%fused_computation.70 | loop fusion | flops 20447232 | bytes 6979616
  139.3 6.4 %bitcast_dynamic-update-slice_fusion.4 = f32[12,32,8,2048]{3,2,1,0:T(8,128)S(1)} fusion(f32[12,32,8,2048]{3,2,1,0:T(8,128)S(1)} %bitcast_dynamic-update-slice_fusion.5, f32[]{:T(128)} %bitcast.39, f32[32,8,2048]{2,1,0:T(8,128)S(1)} %multiply_add_fusion, f32[]{:T(128)} %bitcast.16, f32[]{:T(128)} %bitcast.15, f32[]{:T(128)} %bitcast.14, f32[]{:T(128)} %bitcast.13, ...), kind=kLoop, calls=%fused_computation.69 | loop fusion | flops 20447232 | bytes 6979616
  145.8 6.2 %bitcast_dynamic-update-slice_fusion.3 = f32[12,32,8,2048]{3,2,1,0:T(8,128)S(1)} fusion(f32[12,32,8,2048]{3,2,1,0:T(8,128)S(1)} %bitcast_dynamic-update-slice_fusion.4, f32[]{:T(128)} %bitcast.41, f32[32,8,2048]{2,1,0:T(8,128)S(1)} %multiply_add_fusion, f32[]{:T(128)} %bitcast.22, f32[]{:T(128)} %bitcast.21, f32[]{:T(128)} %bitcast.20, f32[]{:T(128)} %bitcast.19, ...), kind=kLoop, calls=%fused_computation.68 | loop fusion | flops 20447232 | bytes 6979616
  152.0 6.3 %bitcast_dynamic-update-slice_fusion.2 = f32[12,32,8,2048]{3,2,1,0:T(8,128)S(1)} fusion(f32[12,32,8,2048]{3,2,1,0:T(8,128)S(1)} %bitcast_dynamic-update-slice_fusion.3, f32[]{:T(128)} %bitcast.43, f32[32,8,2048]{2,1,0:T(8,128)S(1)} %multiply_add_fusion, f32[]{:T(128)} %bitcast.7, f32[]{:T(128)} %bitcast.6, f32[]{:T(128)} %bitcast.5, f32[]{:T(128)} %bitcast.4, ...), kind=kLoop, calls=%fused_computation.67 | loop fusion | flops 20447232 | bytes 6979616
  158.4 6.3 %bitcast_dynamic-update-slice_fusion.1 = f32[12,32,8,2048]{3,2,1,0:T(8,128)S(1)} fusion(f32[12,32,8,2048]{3,2,1,0:T(8,128)S(1)} %bitcast_dynamic-update-slice_fusion.2, f32[]{:T(128)} %bitcast.48, f32[32,8,2048]{2,1,0:T(8,128)S(1)} %multiply_add_fusion, f32[]{:T(128)} %bitcast.16, f32[]{:T(128)} %bitcast.15, f32[]{:T(128)} %bitcast.14, f32[]{:T(128)} %bitcast.13, ...), kind=kLoop, calls=%fused_computation.66 | loop fusion | flops 20447232 | bytes 6979616
  164.6 6.1 %bitcast_dynamic-update-slice_fusion = f32[12,32,8,2048]{3,2,1,0:T(8,128)S(1)} fusion(f32[12,32,8,2048]{3,2,1,0:T(8,128)S(1)} %bitcast_dynamic-update-slice_fusion.1, f32[]{:T(128)} %bitcast.50, f32[32,8,2048]{2,1,0:T(8,128)S(1)} %multiply_add_fusion, f32[]{:T(128)} %bitcast.22, f32[]{:T(128)} %bitcast.21, f32[]{:T(128)} %bitcast.20, f32[]{:T(128)} %bitcast.19, ...), kind=kLoop, calls=%fused_computation.65 | loop fusion | flops 20447232 | bytes 6979616 | tf_op jit(solution)/shard_map/stack | solution.py:101
  170.8 3.7 %multiply_reduce_fusion = f32[12,8,2048]{2,1,0:T(8,128)S(1)} fusion(f32[12,32,8,2048]{3,2,1,0:T(8,128)S(1)} %bitcast_dynamic-update-slice_fusion, f32[32,8,2048]{2,1,0:T(8,128)S(1)} %pad_multiply_fusion), kind=kLoop, calls=%fused_computation | loop fusion | flops 12386304 | bytes 28049408 | tf_op jit(solution)/shard_map/reduce_sum | solution.py:129
  175.5 86.7 %all-gather.2.cloned.1.call-done = f32[104,8,2048]{2,1,0:T(8,128)} async-done(((f32[13,8,2048]{2,1,0:T(8,128)}), f32[104,8,2048]{2,1,0:T(8,128)}) %all-gather.2.cloned.1.call-update) | async-done | bytes 6815760 | tf_op jit(solution)/shard_map/all_gather | solution.py:160
  (62 shorter events, 38.2 us)
Async XLA Ops:
  6.5 255.6 %all-gather.2.cloned.1.call-start = ((), (), s32[]{:S(2)}) async-start(), calls=%async_computation | async-start | bytes 7667712 | tf_op jit(solution)/shard_map/all_gather | solution.py:160
  7.4 5.7 %collective-permute-start.1 = (f32[1,8,2048]{2,1,0:T(8,128)S(1)}, f32[1,8,2048]{2,1,0:T(8,128)S(1)}, u32[]{:S(2)}, u32[]{:S(2)}) collective-permute-start(f32[1,8,2048]{2,1,0:T(8,128)S(1)} %get-tuple-element.18), channel_id=1, source_target_pairs={{0,32},{32,64},{64,96},{96,128},{128,160},{160,192},{192,224},{1,3... | collective-permute-start | bytes 196616 | tf_op jit(solution)/shard_map/ppermute | solution.py:15
  11.8 5.2 %collective-permute-start = (f32[1,8,2048]{2,1,0:T(8,128)S(1)}, f32[1,8,2048]{2,1,0:T(8,128)S(1)}, u32[]{:S(2)}, u32[]{:S(2)}) collective-permute-start(f32[1,8,2048]{2,1,0:T(8,128)S(1)} %get-tuple-element.17), channel_id=1, source_target_pairs={{32,0},{64,32},{96,64},{128,96},{160,128},{192,160},{224,192},{33,... | collective-permute-start | bytes 196616 | tf_op jit(solution)/shard_map/ppermute | solution.py:17
  13.1 14.6 %copy-start.1 = (f32[32,8,2048]{2,1,0:T(8,128)S(1)}, f32[32,8,2048]{2,1,0:T(8,128)}, u32[]{:S(2)}) copy-start(f32[32,8,2048]{2,1,0:T(8,128)} %param.5) | copy-start | bytes 6291460
  17.4 9.1 %collective-permute-start.2 = (f32[34,1,2048]{2,1,0:T(1,128)S(1)}, f32[34,1,2048]{2,1,0:T(1,128)S(1)}, u32[]{:S(2)}, u32[]{:S(2)}) collective-permute-start(f32[34,1,2048]{2,1,0:T(1,128)S(1)} %get-tuple-element.11), channel_id=1, source_target_pairs={{1,0},{2,1},{3,2},{4,3},{5,4},{6,5},{7,6},{8,7},{9,8},{10,9},{11,1... | collective-permute-start | bytes 835592 | tf_op jit(solution)/shard_map/ppermute | solution.py:17
  21.2 15.8 %copy-start.2 = (f32[4,3]{1,0:T(4,128)S(1)}, f32[4,3]{1,0:T(4,128)}, u32[]{:S(2)}) copy-start(f32[4,3]{1,0:T(4,128)} %param.8) | copy-start | bytes 148
  21.2 6.5 %collective-permute-start.3 = (f32[34,1,2048]{2,1,0:T(1,128)S(1)}, f32[34,1,2048]{2,1,0:T(1,128)S(1)}, u32[]{:S(2)}, u32[]{:S(2)}) collective-permute-start(f32[34,1,2048]{2,1,0:T(1,128)S(1)} %get-tuple-element.12), channel_id=1, source_target_pairs={{0,1},{1,2},{2,3},{3,4},{4,5},{5,6},{6,7},{7,8},{8,9},{9,10},{10,1... | collective-permute-start | bytes 835592 | tf_op jit(solution)/shard_map/ppermute | solution.py:15
  32.1 17.8 %copy-start.5 = (f32[4]{0:T(128)S(1)}, f32[4]{0:T(128)}, u32[]{:S(2)}) copy-start(f32[4]{0:T(128)} %param.7) | copy-start | bytes 52
  32.1 26.0 %copy-start.3 = (f32[3,4]{1,0:T(4,128)S(1)}, f32[3,4]{1,0:T(4,128)}, u32[]{:S(2)}) copy-start(f32[3,4]{1,0:T(4,128)} %param.6) | copy-start | bytes 148
  32.2 26.6 %copy-start.4 = (f32[4,3]{1,0:T(4,128)S(1)}, f32[4,3]{1,0:T(4,128)}, u32[]{:S(2)}) copy-start(f32[4,3]{1,0:T(4,128)} %param.9) | copy-start | bytes 148
  32.2 5.5 %collective-permute-start.5 = (f32[1,8,2048]{2,1,0:T(8,128)S(1)}, f32[1,8,2048]{2,1,0:T(8,128)S(1)}, u32[]{:S(2)}, u32[]{:S(2)}) collective-permute-start(f32[1,8,2048]{2,1,0:T(8,128)S(1)} %get-tuple-element.15), channel_id=1, source_target_pairs={{0,32},{32,64},{64,96},{96,128},{128,160},{160,192},{192,224},{1,3... | collective-permute-start | bytes 196616 | tf_op jit(solution)/shard_map/ppermute | solution.py:15
  35.7 6.3 %collective-permute-start.4 = (f32[1,8,2048]{2,1,0:T(8,128)S(1)}, f32[1,8,2048]{2,1,0:T(8,128)S(1)}, u32[]{:S(2)}, u32[]{:S(2)}) collective-permute-start(f32[1,8,2048]{2,1,0:T(8,128)S(1)} %get-tuple-element.16), channel_id=1, source_target_pairs={{32,0},{64,32},{96,64},{128,96},{160,128},{192,160},{224,192},{33,... | collective-permute-start | bytes 196616 | tf_op jit(solution)/shard_map/ppermute | solution.py:17
  42.4 17.1 %collective-permute-start.6 = (f32[34,1,2048]{2,1,0:T(1,128)S(1)}, f32[34,1,2048]{2,1,0:T(1,128)S(1)}, u32[]{:S(2)}, u32[]{:S(2)}) collective-permute-start(f32[34,1,2048]{2,1,0:T(1,128)S(1)} %get-tuple-element.9), channel_id=1, source_target_pairs={{1,0},{2,1},{3,2},{4,3},{5,4},{6,5},{7,6},{8,7},{9,8},{10,9},{11,1... | collective-permute-start | bytes 835592 | tf_op jit(solution)/shard_map/ppermute | solution.py:17
  44.3 15.2 %collective-permute-start.7 = (f32[34,1,2048]{2,1,0:T(1,128)S(1)}, f32[34,1,2048]{2,1,0:T(1,128)S(1)}, u32[]{:S(2)}, u32[]{:S(2)}) collective-permute-start(f32[34,1,2048]{2,1,0:T(1,128)S(1)} %get-tuple-element.10), channel_id=1, source_target_pairs={{0,1},{1,2},{2,3},{3,4},{4,5},{5,6},{6,7},{7,8},{8,9},{9,10},{10,1... | collective-permute-start | bytes 835592 | tf_op jit(solution)/shard_map/ppermute | solution.py:15
  64.9 19.3 %collective-permute-start.9 = (f32[1,8,2048]{2,1,0:T(8,128)S(1)}, f32[1,8,2048]{2,1,0:T(8,128)S(1)}, u32[]{:S(2)}, u32[]{:S(2)}) collective-permute-start(f32[1,8,2048]{2,1,0:T(8,128)S(1)} %get-tuple-element.13), channel_id=1, source_target_pairs={{0,32},{32,64},{64,96},{96,128},{128,160},{160,192},{192,224},{1,3... | collective-permute-start | bytes 196616 | tf_op jit(solution)/shard_map/ppermute | solution.py:15
  69.8 14.4 %collective-permute-start.8 = (f32[1,8,2048]{2,1,0:T(8,128)S(1)}, f32[1,8,2048]{2,1,0:T(8,128)S(1)}, u32[]{:S(2)}, u32[]{:S(2)}) collective-permute-start(f32[1,8,2048]{2,1,0:T(8,128)S(1)} %get-tuple-element.14), channel_id=1, source_target_pairs={{32,0},{64,32},{96,64},{128,96},{160,128},{192,160},{224,192},{33,... | collective-permute-start | bytes 196616 | tf_op jit(solution)/shard_map/ppermute | solution.py:17
  84.6 7.9 %collective-permute-start.10 = (f32[34,1,2048]{2,1,0:T(1,128)S(1)}, f32[34,1,2048]{2,1,0:T(1,128)S(1)}, u32[]{:S(2)}, u32[]{:S(2)}) collective-permute-start(f32[34,1,2048]{2,1,0:T(1,128)S(1)} %get-tuple-element.7), channel_id=1, source_target_pairs={{1,0},{2,1},{3,2},{4,3},{5,4},{6,5},{7,6},{8,7},{9,8},{10,9},{11,1... | collective-permute-start | bytes 835592 | tf_op jit(solution)/shard_map/ppermute | solution.py:17
  86.5 7.1 %collective-permute-start.11 = (f32[34,1,2048]{2,1,0:T(1,128)S(1)}, f32[34,1,2048]{2,1,0:T(1,128)S(1)}, u32[]{:S(2)}, u32[]{:S(2)}) collective-permute-start(f32[34,1,2048]{2,1,0:T(1,128)S(1)} %get-tuple-element.8), channel_id=1, source_target_pairs={{0,1},{1,2},{2,3},{3,4},{4,5},{5,6},{6,7},{7,8},{8,9},{9,10},{10,1... | collective-permute-start | bytes 835592 | tf_op jit(solution)/shard_map/ppermute | solution.py:15
  263.0 5.1 %copy-start = (f32[104,8,2048]{2,1,0:T(8,128)S(1)}, f32[104,8,2048]{2,1,0:T(8,128)}, u32[]{:S(2)}) copy-start(f32[104,8,2048]{2,1,0:T(8,128)} %all-gather.2.cloned.1.call-done) | copy-start | bytes 20447236
Sparse Core Ops, SparseCore 0:
  175.6 86.4 all-gather.1
where the time goes:
time: 278 us; the launch traced here: 276 us
  other arithmetic  112 us (40%)
  waiting for transfers between devices  99.7 us (36%)
  starting transfers between devices  36.7 us (13%)
  between operations  21.4 us (8%)
  local copies, waits for them, and re-layouts  6.12 us (2%)
    all_gather x1, waiting for transfers between devices, per_device(): lax.all_gather(partial_value, 'depth', axis=0, tiled=True)  86.7 us
    unnamed x11, other arithmetic  70.9 us
    ppermute x6, starting transfers between devices, with_halo(): lax.ppermute(tail, axis, [(i, (i + 1) % count) for i in range(ends)])  25.1 us
    ppermute x6, starting transfers between devices, with_halo(): lax.ppermute(head, axis, [((i + 1) % count, i) for i in range(ends)])  11.5 us
    ppermute x6, waiting for transfers between devices, with_halo(): lax.ppermute(head, axis, [((i + 1) % count, i) for i in range(ends)])  10.7 us
    add x2, other arithmetic, diffuse(): return centre + 0.12 * flux_sum  9.78 us
    mul x1, other arithmetic, render_slab(): weights = before * opacity  8.85 us
    add x7, other arithmetic, over(): return front + (1.0 - front[12:13]) * back  6.42 us
  transfers between devices with their start and end apart: 13, of which 7 were waited for; matrix products, arithmetic and copies ran while one was open for 6% of the time, Pallas kernels for 0%

commit v1 on v0

--- a/solution.py
+++ b/solution.py
@@ -157,9 +157,9 @@
         light_colour,
         alpha_top,
     )
-    gathered = lax.all_gather(partial_value, "depth", axis=0, tiled=True).reshape(
-        depth_count, 13, band_rows, width_cells
-    )
+    gathered = jnp.concatenate(
+        lax.all_to_all(jnp.stack([partial_value] * lax.axis_size("depth")), "depth", 0, 0), axis=0
+    ).reshape(depth_count, 13, band_rows, width_cells)
     forward = gathered[0]
     for slab_index in range(1, depth_count):
         forward = over(forward, gathered[slab_index])

time: 278 us -> 333 us (1.20); the launches traced: 276 us -> 328 us
  blocking collectives: 0 us -> 156 us
  waiting for transfers between devices: 99.7 us -> 13 us
  between operations: 21.4 us -> 8.1 us
  other arithmetic: 112 us -> 107 us
    all_to_all x0 -> x1, blocking collectives: none -> 156 us  [per_device(): lax.all_to_all(jnp.stack([partial_value] * lax.axis_size('depth')), 'dept...]
    all_gather x1 -> x0, waiting for transfers between devices: 86.7 us -> none  [per_device(): lax.all_gather(partial_value, 'depth', axis=0, tiled=True)]
    add x7, other arithmetic: 6.42 us -> 1.72 us  [over(): return front + (1.0 - front[12:13]) * back]
  transfers between devices with their start and end apart: 13 -> 12, of which waited for: 7 -> 6; matrix products, arithmetic and copies ran while one was open for 6% -> 5% of each run, Pallas kernels for 0% -> 0%
where the time goes in v1:
time: 333 us; the launch traced here: 328 us
  blocking collectives  156 us (47%)
  other arithmetic  107 us (32%)
  starting transfers between devices  36.7 us (11%)
  waiting for transfers between devices  13 us (4%)
  between operations  8.1 us (2%)
  local copies, waits for them, and re-layouts  6.97 us (2%)
    all_to_all x1, blocking collectives, per_device(): lax.all_to_all(jnp.stack([partial_value] * lax.axis_size('depth')), 'dept...  156 us
    unnamed x11, other arithmetic  71.4 us
    ppermute x6, starting transfers between devices, with_halo(): lax.ppermute(tail, axis, [(i, (i + 1) % count) for i in range(ends)])  25.1 us
    ppermute x6, starting transfers between devices, with_halo(): lax.ppermute(head, axis, [((i + 1) % count, i) for i in range(ends)])  11.5 us
    ppermute x6, waiting for transfers between devices, with_halo(): lax.ppermute(head, axis, [((i + 1) % count, i) for i in range(ends)])  10.6 us
    add x2, other arithmetic, diffuse(): return centre + 0.12 * flux_sum  9.78 us
    mul x1, other arithmetic, render_slab(): weights = before * opacity  8.85 us
  transfers between devices with their start and end apart: 12, of which 6 were waited for; matrix products, arithmetic and copies ran while one was open for 5% of the time, Pallas kernels for 0%

profile of v1, /device:TPU:1, one launch (start us, length us, event | category | flops | bytes accessed | tf_op | source)
XLA Modules:
  0.0 327.6 jit_solution(10348484469648915697)
XLA Ops:
  0.9 4.4 %collective-permute-start.1 = (f32[1,8,2048]{2,1,0:T(8,128)S(1)}, f32[1,8,2048]{2,1,0:T(8,128)S(1)}, u32[]{:S(2)}, u32[]{:S(2)}) collective-permute-start(f32[1,8,2048]{2,1,0:T(8,128)S(1)} %get-tuple-element.18), channel_id=1, source_target_pairs={{0,32},{32,64},{64,96},{96,128},{128,160},{160,192},{192,224},{1,3... | collective-permute-start | bytes 196616 | tf_op jit(solution)/shard_map/ppermute | solution.py:15
  10.8 3.8 %collective-permute-start.2 = (f32[34,1,2048]{2,1,0:T(1,128)S(1)}, f32[34,1,2048]{2,1,0:T(1,128)S(1)}, u32[]{:S(2)}, u32[]{:S(2)}) collective-permute-start(f32[34,1,2048]{2,1,0:T(1,128)S(1)} %get-tuple-element.11), channel_id=1, source_target_pairs={{1,0},{2,1},{3,2},{4,3},{5,4},{6,5},{7,6},{8,7},{9,8},{10,9},{11,1... | collective-permute-start | bytes 835592 | tf_op jit(solution)/shard_map/ppermute | solution.py:17
  21.2 4.4 %multiply_add_fusion.1 = f32[32,8,2048]{2,1,0:T(8,128)S(1)} fusion(f32[32,8,2048]{2,1,0:T(8,128)S(1)} %copy-done, f32[34,8,2048]{2,1,0:T(8,128)S(1)} %constant_dynamic-update-slice_fusion, f32[34,1,2048]{2,1,0:T(1,128)S(1)} %collective-permute-done.3, f32[34,1,2048]{2,1,0:T(1,128)S(1)} %collective-permute-done.2, ...), kind=kLoop, calls=%fused_computation.87 | loop fusion | flops 18350080 | bytes 7110656 | tf_op jit(solution)/shard_map/add | solution.py:39
  31.2 4.3 %collective-permute-done.4 = f32[1,8,2048]{2,1,0:T(8,128)S(1)} collective-permute-done((f32[1,8,2048]{2,1,0:T(8,128)S(1)}, f32[1,8,2048]{2,1,0:T(8,128)S(1)}, u32[]{:S(2)}, u32[]{:S(2)}) %collective-permute-start.4) | collective-permute-done | bytes 65568 | tf_op jit(solution)/shard_map/ppermute | solution.py:17
  37.8 5.5 %collective-permute-start.7 = (f32[34,1,2048]{2,1,0:T(1,128)S(1)}, f32[34,1,2048]{2,1,0:T(1,128)S(1)}, u32[]{:S(2)}, u32[]{:S(2)}) collective-permute-start(f32[34,1,2048]{2,1,0:T(1,128)S(1)} %get-tuple-element.10), channel_id=1, source_target_pairs={{0,1},{1,2},{2,3},{3,4},{4,5},{5,6},{6,7},{7,8},{8,9},{9,10},{10,1... | collective-permute-start | bytes 835592 | tf_op jit(solution)/shard_map/ppermute | solution.py:15
  53.0 5.4 %multiply_add_fusion = f32[32,8,2048]{2,1,0:T(8,128)S(1)} fusion(f32[32,8,2048]{2,1,0:T(8,128)S(1)} %multiply_add_fusion.1, f32[1,8,2048]{2,1,0:T(8,128)S(1)} %collective-permute-done.4, f32[1,8,2048]{2,1,0:T(8,128)S(1)} %collective-permute-done.5, f32[34,1,2048]{2,1,0:T(1,128)S(1)} %collective-permute-done.7, f32[34,1,2048]{2,1,0:T(1,128)S(1)} %collective-permute-done.6), kind=kLoop, calls=%fused_computation.86 | loop fusion | flops 20447232 | bytes 4882432 | tf_op jit(solution)/shard_map/add | solution.py:39
  58.4 4.9 %collective-permute-start.9 = (f32[1,8,2048]{2,1,0:T(8,128)S(1)}, f32[1,8,2048]{2,1,0:T(8,128)S(1)}, u32[]{:S(2)}, u32[]{:S(2)}) collective-permute-start(f32[1,8,2048]{2,1,0:T(8,128)S(1)} %get-tuple-element.13), channel_id=1, source_target_pairs={{0,32},{32,64},{64,96},{96,128},{128,160},{160,192},{192,224},{1,3... | collective-permute-start | bytes 196616 | tf_op jit(solution)/shard_map/ppermute | solution.py:15
  64.6 4.1 %fusion.33 = f32[32,8,2048]{2,1,0:T(8,128)S(1)} fusion(f32[32,8,2048]{2,1,0:T(8,128)S(1)} %multiply_add_fusion, f32[]{:T(128)} %bitcast.3, f32[]{:T(128)} %bitcast.2, f32[]{:T(128)} %bitcast.1, f32[]{:T(128)} %bitcast), kind=kOutput, calls=%fused_computation.83 | output fusion | flops 23068672 | bytes 4194320 | tf_op jit(solution)/shard_map/jit(cumprod)/reduce_window | solution.py:126
  68.9 8.9 %pad_multiply_fusion = f32[32,8,2048]{2,1,0:T(8,128)S(1)} fusion(f32[31,8,2048]{2,1,0:T(8,128)S(1)} %slice.366, f32[]{:T(128)} %bitcast.3, f32[]{:T(128)} %bitcast.2, f32[]{:T(128)} %bitcast.1, f32[]{:T(128)} %bitcast, f32[32,8,2048]{2,1,0:T(8,128)S(1)} %multiply_add_fusion.1, f32[1,8,2048]{2,1,0:T(8,128)S(1)} %collective-permute-done.4, ...), kind=kLoop, calls=%fused_computation.82 | loop fusion | flops 27262976 | bytes 6914064 | tf_op jit(solution)/shard_map/mul | solution.py:128
  80.1 3.8 %collective-permute-start.11 = (f32[34,1,2048]{2,1,0:T(1,128)S(1)}, f32[34,1,2048]{2,1,0:T(1,128)S(1)}, u32[]{:S(2)}, u32[]{:S(2)}) collective-permute-start(f32[34,1,2048]{2,1,0:T(1,128)S(1)} %get-tuple-element.8), channel_id=1, source_target_pairs={{0,1},{1,2},{2,3},{3,4},{4,5},{5,6},{6,7},{7,8},{8,9},{9,10},{10,1... | collective-permute-start | bytes 835592 | tf_op jit(solution)/shard_map/ppermute | solution.py:15
  87.2 7.9 %bitcast_dynamic-update-slice_fusion.11 = (f32[12,32,8,2048]{3,2,1,0:T(8,128)S(1)}, f32[32,8,2048]{2,1,0:T(8,128)S(1)}) fusion(f32[]{:T(128)} %bitcast.8, f32[32,8,2048]{2,1,0:T(8,128)S(1)} %multiply_add_fusion, f32[]{:T(128)} %bitcast.7, f32[]{:T(128)} %bitcast.6, f32[]{:T(128)} %bitcast.5, f32[]{:T(128)} %bitcast.4, f32[]{:T(128)} %bitcast.11, ...), kind=kLoop, calls=%fused_computation.76 | loop fusion | flops 20971520 | bytes 6979616
  95.1 6.3 %bitcast_dynamic-update-slice_fusion.10 = f32[12,32,8,2048]{3,2,1,0:T(8,128)S(1)} fusion(f32[12,32,8,2048]{3,2,1,0:T(8,128)S(1)} %get-tuple-element.5, f32[]{:T(128)} %bitcast.17, f32[32,8,2048]{2,1,0:T(8,128)S(1)} %multiply_add_fusion, f32[]{:T(128)} %bitcast.16, f32[]{:T(128)} %bitcast.15, f32[]{:T(128)} %bitcast.14, f32[]{:T(128)} %bitcast.13, ...), kind=kLoop, calls=%fused_computation.75 | loop fusion | flops 20447232 | bytes 6979616
  101.5 6.5 %bitcast_dynamic-update-slice_fusion.9 = f32[12,32,8,2048]{3,2,1,0:T(8,128)S(1)} fusion(f32[12,32,8,2048]{3,2,1,0:T(8,128)S(1)} %bitcast_dynamic-update-slice_fusion.10, f32[]{:T(128)} %bitcast.23, f32[32,8,2048]{2,1,0:T(8,128)S(1)} %multiply_add_fusion, f32[]{:T(128)} %bitcast.22, f32[]{:T(128)} %bitcast.21, f32[]{:T(128)} %bitcast.20, f32[]{:T(128)} %bitcast.19, ...), kind=kLoop, calls=%fused_computation.74 | loop fusion | flops 20447232 | bytes 6979616
  107.9 6.2 %bitcast_dynamic-update-slice_fusion.8 = f32[12,32,8,2048]{3,2,1,0:T(8,128)S(1)} fusion(f32[12,32,8,2048]{3,2,1,0:T(8,128)S(1)} %bitcast_dynamic-update-slice_fusion.9, f32[]{:T(128)} %bitcast.25, f32[32,8,2048]{2,1,0:T(8,128)S(1)} %multiply_add_fusion, f32[]{:T(128)} %bitcast.7, f32[]{:T(128)} %bitcast.6, f32[]{:T(128)} %bitcast.5, f32[]{:T(128)} %bitcast.4, ...), kind=kLoop, calls=%fused_computation.73 | loop fusion | flops 20447232 | bytes 6979616
  114.2 6.3 %bitcast_dynamic-update-slice_fusion.7 = f32[12,32,8,2048]{3,2,1,0:T(8,128)S(1)} fusion(f32[12,32,8,2048]{3,2,1,0:T(8,128)S(1)} %bitcast_dynamic-update-slice_fusion.8, f32[]{:T(128)} %bitcast.30, f32[32,8,2048]{2,1,0:T(8,128)S(1)} %multiply_add_fusion, f32[]{:T(128)} %bitcast.16, f32[]{:T(128)} %bitcast.15, f32[]{:T(128)} %bitcast.14, f32[]{:T(128)} %bitcast.13, ...), kind=kLoop, calls=%fused_computation.72 | loop fusion | flops 20447232 | bytes 6979616
  120.5 6.4 %bitcast_dynamic-update-slice_fusion.6 = f32[12,32,8,2048]{3,2,1,0:T(8,128)S(1)} fusion(f32[12,32,8,2048]{3,2,1,0:T(8,128)S(1)} %bitcast_dynamic-update-slice_fusion.7, f32[]{:T(128)} %bitcast.32, f32[32,8,2048]{2,1,0:T(8,128)S(1)} %multiply_add_fusion, f32[]{:T(128)} %bitcast.22, f32[]{:T(128)} %bitcast.21, f32[]{:T(128)} %bitcast.20, f32[]{:T(128)} %bitcast.19, ...), kind=kLoop, calls=%fused_computation.71 | loop fusion | flops 20447232 | bytes 6979616
  126.9 6.3 %bitcast_dynamic-update-slice_fusion.5 = f32[12,32,8,2048]{3,2,1,0:T(8,128)S(1)} fusion(f32[12,32,8,2048]{3,2,1,0:T(8,128)S(1)} %bitcast_dynamic-update-slice_fusion.6, f32[]{:T(128)} %bitcast.34, f32[32,8,2048]{2,1,0:T(8,128)S(1)} %multiply_add_fusion, f32[]{:T(128)} %bitcast.7, f32[]{:T(128)} %bitcast.6, f32[]{:T(128)} %bitcast.5, f32[]{:T(128)} %bitcast.4, ...), kind=kLoop, calls=%fused_computation.70 | loop fusion | flops 20447232 | bytes 6979616
  133.2 6.4 %bitcast_dynamic-update-slice_fusion.4 = f32[12,32,8,2048]{3,2,1,0:T(8,128)S(1)} fusion(f32[12,32,8,2048]{3,2,1,0:T(8,128)S(1)} %bitcast_dynamic-update-slice_fusion.5, f32[]{:T(128)} %bitcast.39, f32[32,8,2048]{2,1,0:T(8,128)S(1)} %multiply_add_fusion, f32[]{:T(128)} %bitcast.16, f32[]{:T(128)} %bitcast.15, f32[]{:T(128)} %bitcast.14, f32[]{:T(128)} %bitcast.13, ...), kind=kLoop, calls=%fused_computation.69 | loop fusion | flops 20447232 | bytes 6979616
  139.7 6.4 %bitcast_dynamic-update-slice_fusion.3 = f32[12,32,8,2048]{3,2,1,0:T(8,128)S(1)} fusion(f32[12,32,8,2048]{3,2,1,0:T(8,128)S(1)} %bitcast_dynamic-update-slice_fusion.4, f32[]{:T(128)} %bitcast.41, f32[32,8,2048]{2,1,0:T(8,128)S(1)} %multiply_add_fusion, f32[]{:T(128)} %bitcast.22, f32[]{:T(128)} %bitcast.21, f32[]{:T(128)} %bitcast.20, f32[]{:T(128)} %bitcast.19, ...), kind=kLoop, calls=%fused_computation.68 | loop fusion | flops 20447232 | bytes 6979616
  146.1 6.2 %bitcast_dynamic-update-slice_fusion.2 = f32[12,32,8,2048]{3,2,1,0:T(8,128)S(1)} fusion(f32[12,32,8,2048]{3,2,1,0:T(8,128)S(1)} %bitcast_dynamic-update-slice_fusion.3, f32[]{:T(128)} %bitcast.43, f32[32,8,2048]{2,1,0:T(8,128)S(1)} %multiply_add_fusion, f32[]{:T(128)} %bitcast.7, f32[]{:T(128)} %bitcast.6, f32[]{:T(128)} %bitcast.5, f32[]{:T(128)} %bitcast.4, ...), kind=kLoop, calls=%fused_computation.67 | loop fusion | flops 20447232 | bytes 6979616
  152.3 6.3 %bitcast_dynamic-update-slice_fusion.1 = f32[12,32,8,2048]{3,2,1,0:T(8,128)S(1)} fusion(f32[12,32,8,2048]{3,2,1,0:T(8,128)S(1)} %bitcast_dynamic-update-slice_fusion.2, f32[]{:T(128)} %bitcast.48, f32[32,8,2048]{2,1,0:T(8,128)S(1)} %multiply_add_fusion, f32[]{:T(128)} %bitcast.16, f32[]{:T(128)} %bitcast.15, f32[]{:T(128)} %bitcast.14, f32[]{:T(128)} %bitcast.13, ...), kind=kLoop, calls=%fused_computation.66 | loop fusion | flops 20447232 | bytes 6979616
  158.6 6.5 %bitcast_dynamic-update-slice_fusion = f32[12,32,8,2048]{3,2,1,0:T(8,128)S(1)} fusion(f32[12,32,8,2048]{3,2,1,0:T(8,128)S(1)} %bitcast_dynamic-update-slice_fusion.1, f32[]{:T(128)} %bitcast.50, f32[32,8,2048]{2,1,0:T(8,128)S(1)} %multiply_add_fusion, f32[]{:T(128)} %bitcast.22, f32[]{:T(128)} %bitcast.21, f32[]{:T(128)} %bitcast.20, f32[]{:T(128)} %bitcast.19, ...), kind=kLoop, calls=%fused_computation.65 | loop fusion | flops 20447232 | bytes 6979616 | tf_op jit(solution)/shard_map/stack | solution.py:101
  165.1 3.7 %multiply_reduce_fusion = f32[12,8,2048]{2,1,0:T(8,128)S(1)} fusion(f32[12,32,8,2048]{3,2,1,0:T(8,128)S(1)} %bitcast_dynamic-update-slice_fusion, f32[32,8,2048]{2,1,0:T(8,128)S(1)} %pad_multiply_fusion), kind=kLoop, calls=%fused_computation | loop fusion | flops 12386304 | bytes 28049408 | tf_op jit(solution)/shard_map/reduce_sum | solution.py:129
  169.7 156.0 %all_to_all.5 = f32[8,13,8,2048]{3,2,1,0:T(8,128)S(1)} all-to-all(f32[8,13,8,2048]{3,2,1,0:T(8,128)S(1)} %stack.63), channel_id=1, replica_groups=mesh['depth'=8,'height'=32] {'depth'}, dimensions={0} | all-to-all | bytes 13631488 | tf_op jit(solution)/shard_map/all_to_all | solution.py:161
  (59 shorter events, 32.6 us)
Async XLA Ops:
  0.9 5.7 %collective-permute-start.1 = (f32[1,8,2048]{2,1,0:T(8,128)S(1)}, f32[1,8,2048]{2,1,0:T(8,128)S(1)}, u32[]{:S(2)}, u32[]{:S(2)}) collective-permute-start(f32[1,8,2048]{2,1,0:T(8,128)S(1)} %get-tuple-element.18), channel_id=1, source_target_pairs={{0,32},{32,64},{64,96},{96,128},{128,160},{160,192},{192,224},{1,3... | collective-permute-start | bytes 196616 | tf_op jit(solution)/shard_map/ppermute | solution.py:15
  5.3 5.2 %collective-permute-start = (f32[1,8,2048]{2,1,0:T(8,128)S(1)}, f32[1,8,2048]{2,1,0:T(8,128)S(1)}, u32[]{:S(2)}, u32[]{:S(2)}) collective-permute-start(f32[1,8,2048]{2,1,0:T(8,128)S(1)} %get-tuple-element.17), channel_id=1, source_target_pairs={{32,0},{64,32},{96,64},{128,96},{160,128},{192,160},{224,192},{33,... | collective-permute-start | bytes 196616 | tf_op jit(solution)/shard_map/ppermute | solution.py:17
  6.6 14.6 %copy-start = (f32[32,8,2048]{2,1,0:T(8,128)S(1)}, f32[32,8,2048]{2,1,0:T(8,128)}, u32[]{:S(2)}) copy-start(f32[32,8,2048]{2,1,0:T(8,128)} %param.5) | copy-start | bytes 6291460
  10.8 9.1 %collective-permute-start.2 = (f32[34,1,2048]{2,1,0:T(1,128)S(1)}, f32[34,1,2048]{2,1,0:T(1,128)S(1)}, u32[]{:S(2)}, u32[]{:S(2)}) collective-permute-start(f32[34,1,2048]{2,1,0:T(1,128)S(1)} %get-tuple-element.11), channel_id=1, source_target_pairs={{1,0},{2,1},{3,2},{4,3},{5,4},{6,5},{7,6},{8,7},{9,8},{10,9},{11,1... | collective-permute-start | bytes 835592 | tf_op jit(solution)/shard_map/ppermute | solution.py:17
  14.7 15.8 %copy-start.1 = (f32[4,3]{1,0:T(4,128)S(1)}, f32[4,3]{1,0:T(4,128)}, u32[]{:S(2)}) copy-start(f32[4,3]{1,0:T(4,128)} %param.8) | copy-start | bytes 148
  14.7 6.5 %collective-permute-start.3 = (f32[34,1,2048]{2,1,0:T(1,128)S(1)}, f32[34,1,2048]{2,1,0:T(1,128)S(1)}, u32[]{:S(2)}, u32[]{:S(2)}) collective-permute-start(f32[34,1,2048]{2,1,0:T(1,128)S(1)} %get-tuple-element.12), channel_id=1, source_target_pairs={{0,1},{1,2},{2,3},{3,4},{4,5},{5,6},{6,7},{7,8},{8,9},{9,10},{10,1... | collective-permute-start | bytes 835592 | tf_op jit(solution)/shard_map/ppermute | solution.py:15
  25.6 17.8 %copy-start.4 = (f32[4]{0:T(128)S(1)}, f32[4]{0:T(128)}, u32[]{:S(2)}) copy-start(f32[4]{0:T(128)} %param.7) | copy-start | bytes 52
  25.6 26.0 %copy-start.2 = (f32[3,4]{1,0:T(4,128)S(1)}, f32[3,4]{1,0:T(4,128)}, u32[]{:S(2)}) copy-start(f32[3,4]{1,0:T(4,128)} %param.6) | copy-start | bytes 148
  25.6 26.7 %copy-start.3 = (f32[4,3]{1,0:T(4,128)S(1)}, f32[4,3]{1,0:T(4,128)}, u32[]{:S(2)}) copy-start(f32[4,3]{1,0:T(4,128)} %param.9) | copy-start | bytes 148
  25.6 5.6 %collective-permute-start.5 = (f32[1,8,2048]{2,1,0:T(8,128)S(1)}, f32[1,8,2048]{2,1,0:T(8,128)S(1)}, u32[]{:S(2)}, u32[]{:S(2)}) collective-permute-start(f32[1,8,2048]{2,1,0:T(8,128)S(1)} %get-tuple-element.15), channel_id=1, source_target_pairs={{0,32},{32,64},{64,96},{96,128},{128,160},{160,192},{192,224},{1,3... | collective-permute-start | bytes 196616 | tf_op jit(solution)/shard_map/ppermute | solution.py:15
  29.2 6.3 %collective-permute-start.4 = (f32[1,8,2048]{2,1,0:T(8,128)S(1)}, f32[1,8,2048]{2,1,0:T(8,128)S(1)}, u32[]{:S(2)}, u32[]{:S(2)}) collective-permute-start(f32[1,8,2048]{2,1,0:T(8,128)S(1)} %get-tuple-element.16), channel_id=1, source_target_pairs={{32,0},{64,32},{96,64},{128,96},{160,128},{192,160},{224,192},{33,... | collective-permute-start | bytes 196616 | tf_op jit(solution)/shard_map/ppermute | solution.py:17
  35.9 17.1 %collective-permute-start.6 = (f32[34,1,2048]{2,1,0:T(1,128)S(1)}, f32[34,1,2048]{2,1,0:T(1,128)S(1)}, u32[]{:S(2)}, u32[]{:S(2)}) collective-permute-start(f32[34,1,2048]{2,1,0:T(1,128)S(1)} %get-tuple-element.9), channel_id=1, source_target_pairs={{1,0},{2,1},{3,2},{4,3},{5,4},{6,5},{7,6},{8,7},{9,8},{10,9},{11,1... | collective-permute-start | bytes 835592 | tf_op jit(solution)/shard_map/ppermute | solution.py:17
  37.8 15.2 %collective-permute-start.7 = (f32[34,1,2048]{2,1,0:T(1,128)S(1)}, f32[34,1,2048]{2,1,0:T(1,128)S(1)}, u32[]{:S(2)}, u32[]{:S(2)}) collective-permute-start(f32[34,1,2048]{2,1,0:T(1,128)S(1)} %get-tuple-element.10), channel_id=1, source_target_pairs={{0,1},{1,2},{2,3},{3,4},{4,5},{5,6},{6,7},{7,8},{8,9},{9,10},{10,1... | collective-permute-start | bytes 835592 | tf_op jit(solution)/shard_map/ppermute | solution.py:15
  58.4 19.3 %collective-permute-start.9 = (f32[1,8,2048]{2,1,0:T(8,128)S(1)}, f32[1,8,2048]{2,1,0:T(8,128)S(1)}, u32[]{:S(2)}, u32[]{:S(2)}) collective-permute-start(f32[1,8,2048]{2,1,0:T(8,128)S(1)} %get-tuple-element.13), channel_id=1, source_target_pairs={{0,32},{32,64},{64,96},{96,128},{128,160},{160,192},{192,224},{1,3... | collective-permute-start | bytes 196616 | tf_op jit(solution)/shard_map/ppermute | solution.py:15
  63.3 14.4 %collective-permute-start.8 = (f32[1,8,2048]{2,1,0:T(8,128)S(1)}, f32[1,8,2048]{2,1,0:T(8,128)S(1)}, u32[]{:S(2)}, u32[]{:S(2)}) collective-permute-start(f32[1,8,2048]{2,1,0:T(8,128)S(1)} %get-tuple-element.14), channel_id=1, source_target_pairs={{32,0},{64,32},{96,64},{128,96},{160,128},{192,160},{224,192},{33,... | collective-permute-start | bytes 196616 | tf_op jit(solution)/shard_map/ppermute | solution.py:17
  78.1 7.9 %collective-permute-start.10 = (f32[34,1,2048]{2,1,0:T(1,128)S(1)}, f32[34,1,2048]{2,1,0:T(1,128)S(1)}, u32[]{:S(2)}, u32[]{:S(2)}) collective-permute-start(f32[34,1,2048]{2,1,0:T(1,128)S(1)} %get-tuple-element.7), channel_id=1, source_target_pairs={{1,0},{2,1},{3,2},{4,3},{5,4},{6,5},{7,6},{8,7},{9,8},{10,9},{11,1... | collective-permute-start | bytes 835592 | tf_op jit(solution)/shard_map/ppermute | solution.py:17
  80.1 7.1 %collective-permute-start.11 = (f32[34,1,2048]{2,1,0:T(1,128)S(1)}, f32[34,1,2048]{2,1,0:T(1,128)S(1)}, u32[]{:S(2)}, u32[]{:S(2)}) collective-permute-start(f32[34,1,2048]{2,1,0:T(1,128)S(1)} %get-tuple-element.8), channel_id=1, source_target_pairs={{0,1},{1,2},{2,3},{3,4},{4,5},{5,6},{6,7},{7,8},{8,9},{9,10},{10,1... | collective-permute-start | bytes 835592 | tf_op jit(solution)/shard_map/ppermute | solution.py:15
